TPU v7x, 32 devices: a whole 2x2x4 slice. The times are simulated.
32 devices in a mesh: ctx: 8 (over y, x, core), tp: 4 (over z).
Axes of the slice: x: 2, y: 2, z: 4, core: 2. Of those that a mesh axis runs over, the one named last changes fastest.
Arguments:
- x_gate: bfloat16 [1024, 2048], P('ctx', 'tp'), may hold values from -6 to 6
- x_post: bfloat16 [1024, 2048], P('ctx', 'tp'), may hold values from -6 to 6
- values: bfloat16 [1024, 2048], P('ctx', 'tp'), may hold values from -6 to 6
- decay: float32 [2, 2048, 16], P(None, 'tp'), may hold values from 0.00024414062 to 0.05
- residue: float32 [2, 2048, 16], P(None, 'tp'), may hold values from -4 to 4
- w_out: bfloat16 [2048, 2048], P(('tp', 'ctx')), may hold values from -0.125 to 0.125
Outputs:
- projected: bfloat16 [1024, 2048], P('ctx', 'tp')
All inputs are finite; a program needn't handle non-finite values.
Results may differ from a plain program's by a relative error of at most 0.015.
Values may be sent and summed in bfloat16 or wider, within the bound.
No kernel may reach another device: no remote copies, remote signals or barrier semaphores. Data moves between devices by JAX's collectives and lax.ppermute only.
A program may use at most 128 MiB of HBM per device.

v0:
```python
import functools
import math

import jax
import jax.numpy as jnp
from jax import lax
from jax.experimental import pallas as pl
from jax.experimental.pallas import tpu as pltpu
from jax.sharding import PartitionSpec as P

HIGHEST = lax.Precision.HIGHEST


def partner(value, axis, bit):
    mask = 2**bit
    pairs = [(source, source ^ mask) for source in range(lax.axis_size(axis))]
    return lax.ppermute(value, axis, pairs)


def radices(length_all):
    last_radix = min(128, length_all // 4)
    first_radix = min(32, length_all // last_radix)
    return (first_radix, length_all // (first_radix * last_radix), last_radix)


def rotation(row_count, col_count, modulus):
    product = (
        lax.broadcasted_iota(jnp.int32, (row_count, col_count), 0)
        * lax.broadcasted_iota(jnp.int32, (row_count, col_count), 1)
        % modulus
    )
    angle = product.astype(jnp.float32) * (2.0 * math.pi / modulus)
    return (jnp.cos(angle), -jnp.sin(angle))


def tables(radix_sizes):
    first_radix, mid_radix, last_radix = radix_sizes
    length_all = first_radix * mid_radix * last_radix
    outer_real, outer_imag = rotation(first_radix, first_radix, first_radix)
    mid_real, mid_imag = rotation(mid_radix, mid_radix, mid_radix)
    last_real, last_imag = rotation(last_radix, last_radix, last_radix)
    twist_real, twist_imag = rotation(first_radix, mid_radix * last_radix, length_all)
    twist_real = twist_real.reshape(first_radix, mid_radix, last_radix)
    twist_imag = twist_imag.reshape(first_radix, mid_radix, last_radix)
    inner_real, inner_imag = rotation(mid_radix, last_radix, mid_radix * last_radix)
    return (
        outer_real,
        outer_imag,
        mid_real,
        mid_imag,
        last_real,
        last_imag,
        twist_real,
        twist_imag,
        inner_real,
        inner_imag,
    )


def apply_matrix(pattern, real_part, imag_part, matrix_real, matrix_imag):
    out_real = jnp.einsum(pattern, real_part, matrix_real, precision=HIGHEST) - jnp.einsum(
        pattern, imag_part, matrix_imag, precision=HIGHEST
    )
    out_imag = jnp.einsum(pattern, real_part, matrix_imag, precision=HIGHEST) + jnp.einsum(
        pattern, imag_part, matrix_real, precision=HIGHEST
    )
    return (out_real, out_imag)


def complex_times(left_real, left_imag, right_real, right_imag):
    return (
        left_real * right_real - left_imag * right_imag,
        left_real * right_imag + left_imag * right_real,
    )


def forward(real_part, imag_part, table_set, radix_sizes):
    first_radix, mid_radix, last_radix = radix_sizes
    half_first = first_radix // 2
    batch_rows = real_part.shape[0]
    (
        outer_real,
        outer_imag,
        mid_real,
        mid_imag,
        last_real,
        last_imag,
        twist_real,
        twist_imag,
        inner_real,
        inner_imag,
    ) = table_set
    real_part = real_part.reshape(batch_rows, half_first, mid_radix, last_radix)
    imag_part = imag_part.reshape(batch_rows, half_first, mid_radix, last_radix)
    real_part, imag_part = apply_matrix(
        "banm,ak->bknm", real_part, imag_part, outer_real[:half_first], outer_imag[:half_first]
    )
    real_part, imag_part = complex_times(real_part, imag_part, twist_real, twist_imag)
    real_part, imag_part = apply_matrix("bknm,nj->bkjm", real_part, imag_part, mid_real, mid_imag)
    real_part, imag_part = complex_times(real_part, imag_part, inner_real, inner_imag)
    return apply_matrix("bkjm,mq->bkjq", real_part, imag_part, last_real, last_imag)


def inverse(real_part, imag_part, table_set, radix_sizes):
    first_radix, mid_radix, last_radix = radix_sizes
    half_first = first_radix // 2
    batch_rows = real_part.shape[0]
    (
        outer_real,
        outer_imag,
        mid_real,
        mid_imag,
        last_real,
        last_imag,
        twist_real,
        twist_imag,
        inner_real,
        inner_imag,
    ) = table_set
    real_part, imag_part = apply_matrix(
        "bkjq,mq->bkjm", real_part, imag_part, last_real / last_radix, -last_imag / last_radix
    )
    real_part, imag_part = complex_times(real_part, imag_part, inner_real, -inner_imag)
    real_part, imag_part = apply_matrix(
        "bkjm,nj->bknm", real_part, imag_part, mid_real / mid_radix, -mid_imag / mid_radix
    )
    real_part, imag_part = complex_times(real_part, imag_part, twist_real, -twist_imag)
    matrix_real = outer_real[:half_first] / first_radix
    matrix_imag = -outer_imag[:half_first] / first_radix
    out_real, out_imag = apply_matrix(
        "bknm,ak->banm", real_part, imag_part, matrix_real, matrix_imag
    )
    return (out_real.reshape(batch_rows, -1), out_imag.reshape(batch_rows, -1))


def spectrum(decay_rows, residue_rows, radix_sizes, seq_length):
    first_radix, mid_radix, last_radix = radix_sizes
    length_all = first_radix * mid_radix * last_radix
    poles = decay_rows.shape[1]
    shape_all = (first_radix, mid_radix, last_radix)
    frequency = (
        lax.broadcasted_iota(jnp.int32, shape_all, 0)
        + first_radix * lax.broadcasted_iota(jnp.int32, shape_all, 1)
        + first_radix * mid_radix * lax.broadcasted_iota(jnp.int32, shape_all, 2)
    )
    half_angle = frequency.astype(jnp.float32) * (math.pi / length_all)
    sin_half = jnp.sin(half_angle)
    sin_full = jnp.sin(2.0 * half_angle)
    parity_sign = (1 - 2 * (frequency % 2)).astype(jnp.float32)

    def add_pole(pole_index, running):
        run_real, run_imag = running
        rate_col = lax.dynamic_slice_in_dim(decay_rows, pole_index, 1, 1).reshape(-1, 1, 1, 1)
        weight = lax.dynamic_slice_in_dim(residue_rows, pole_index, 1, 1).reshape(
            -1, 1, 1, 1
        ) * jnp.sqrt(2.0 * rate_col / poles)
        retained = jnp.exp(-rate_col)
        den_real = -jnp.expm1(-rate_col) + 2.0 * retained * sin_half * sin_half
        den_imag = retained * sin_full
        pole_scale = (
            weight
            * (1.0 - jnp.exp(-rate_col * seq_length) * parity_sign)
            / (den_real * den_real + den_imag * den_imag)
        )
        return (run_real + pole_scale * den_real, run_imag - pole_scale * den_imag)

    zeros_all = jnp.zeros((decay_rows.shape[0],) + shape_all, jnp.float32)
    return lax.fori_loop(0, poles, add_pole, (zeros_all, zeros_all))


def general(x_gate, x_post, values, decay, residue, w_out):
    tok_rows, block_width = x_gate.shape
    ctx_count = lax.axis_size("ctx")
    tp_count = lax.axis_size("tp")
    chan_group = block_width // ctx_count
    seq_length = tok_rows * ctx_count
    radix_sizes = radices(2 * seq_length)
    table_set = tables(radix_sizes)
    first_row = lax.axis_index("ctx") * chan_group
    own_rate = lax.dynamic_slice_in_dim(decay, first_row, chan_group, 1)
    own_residue = lax.dynamic_slice_in_dim(residue, first_row, chan_group, 1)
    own_spec = [
        spectrum(own_rate[filter_index], own_residue[filter_index], radix_sizes, seq_length)
        for filter_index in range(2)
    ]
    forward_rows = [x_gate, values] + [x_post]
    row_count = len(forward_rows)
    base_rows = jnp.stack(forward_rows)
    copied = base_rows
    for bit_index in range(tp_count.bit_length() - 1):
        copied = partner(copied, "tp", bit_index)
    sent_rows = jnp.concatenate([base_rows, copied[:, :, ::-1]], axis=0)
    received = lax.all_to_all(
        jnp.swapaxes(sent_rows, 1, 2), "ctx", split_axis=1, concat_axis=2, tiled=True
    )
    gate_fwd = received[0].astype(jnp.float32)
    value_fwd = received[1].astype(jnp.float32)
    mirrored = received[row_count:, :, ::-1].astype(jnp.float32)
    spec_real, spec_imag = forward(value_fwd, mirrored[1], table_set, radix_sizes)
    spec_real, spec_imag = complex_times(spec_real, spec_imag, own_spec[0][0], own_spec[0][1])
    along_fwd, along_rev = inverse(spec_real, spec_imag, table_set, radix_sizes)
    spec_real, spec_imag = forward(
        gate_fwd * along_fwd, mirrored[0] * along_rev, table_set, radix_sizes
    )
    spec_real, spec_imag = complex_times(spec_real, spec_imag, own_spec[1][0], own_spec[1][1])
    sum_fwd, sum_rev = inverse(spec_real, spec_imag, table_set, radix_sizes)
    sum_fwd = received[2].astype(jnp.float32) * sum_fwd
    sum_rev = mirrored[2] * sum_rev
    results = jnp.stack([sum_fwd, sum_rev[:, ::-1]])
    returned = lax.all_to_all(
        results.astype(jnp.bfloat16), "ctx", split_axis=2, concat_axis=1, tiled=True
    ).astype(results.dtype)
    flipped = returned[1, ::-1, :]
    for bit_index in range(tp_count.bit_length() - 1):
        flipped = partner(flipped.astype(jnp.bfloat16), "tp", bit_index).astype(flipped.dtype)
    total_rows = returned[0] + flipped
    total_rows = total_rows.T
    mixed_rows = total_rows.astype(jnp.bfloat16)
    whole_rows = lax.all_gather(mixed_rows, "tp", axis=1, tiled=True)
    projected = lax.dot_general(
        whole_rows,
        lax.all_gather(w_out, "ctx", axis=0, tiled=True),
        (((1,), (1,)), ((), ())),
        preferred_element_type=jnp.float32,
    )
    return projected.astype(jnp.bfloat16)


def cycle(row_factor, col_factor, modulus):
    quarter = modulus // 4
    turned = row_factor * col_factor + quarter // 2
    quadrant = turned // quarter % 4
    angle = (turned % quarter - quarter // 2).astype(jnp.float32) * (2.0 * math.pi / modulus)
    square = angle * angle

    def series(first):
        total = jnp.zeros_like(square)
        for power in range(first + 10, first, -2):
            total = (total + (-1.0) ** ((power - first) // 2) / math.factorial(power)) * square
        return total

    cos = 1.0 + series(0)
    sin = angle + angle * series(1)
    odd = quadrant % 2 == 1
    cos, sin = jnp.where(odd, sin, cos), jnp.where(odd, cos, sin)
    return jnp.where((quadrant == 1) | (quadrant == 2), -cos, cos), jnp.where(quadrant >= 2, -sin, sin)


def put_tables(table_ref, back_ref):
    block = back_ref.shape[1]
    modulus = 4 * block
    coarse = 16
    rows = lax.broadcasted_iota(jnp.int32, (coarse, block), 0)
    cols = lax.broadcasted_iota(jnp.int32, (coarse, block), 1)

    def parts(big, small):
        for place in range(block // coarse):
            big_cos, big_sin = (part[place : place + 1] for part in big)
            cos = halves(big_cos * small[0] - big_sin * small[1])
            sin = halves(-(big_sin * small[0] + big_cos * small[1]))
            yield place * coarse, cos, sin

    def put(ref, first, columns, value):
        ref[first : first + coarse, columns] = value[0]
        low = first + ref.shape[0] // 2
        ref[low : low + coarse, columns] = value[1]

    frequency = 2 * cols + 1
    for first, cos, sin in parts(cycle(coarse * rows, frequency, modulus), cycle(rows, frequency, modulus)):
        put(table_ref, first, slice(0, block), cos)
        put(table_ref, first, slice(block, 2 * block), sin)
    for first, cos, sin in parts(cycle(2 * coarse * rows, cols, modulus), cycle(2 * rows + 1, cols, modulus)):
        put(back_ref, first, slice(0, block), cos)
        put(back_ref, block + first, slice(0, block), sin)


def halves(value):
    high = value.astype(jnp.bfloat16)
    return high, (value - high.astype(jnp.float32)).astype(jnp.bfloat16)


def mul(left, right):
    return jnp.dot(left, right, preferred_element_type=jnp.float32)


def mul3(high, low, table_ref):
    left = jnp.concatenate([high, high, low], axis=1)
    return mul(left, jnp.concatenate([table_ref[...], table_ref[: table_ref.shape[0] // 2]], axis=0))


def mul2(value, table_ref):
    return mul(jnp.concatenate([value, value], axis=1), table_ref[...])


def pack_kernel(
    gate_hbm, value_hbm, post_hbm, decay_hbm, residue_hbm,
    out_hbm, own_hbm, sent_hbm, held_ref, cut_ref, ready_ref, sems, out_sems,
):
    ctx_count, _, group, tok = out_hbm.shape
    width = gate_hbm.shape[1]
    half = decay_hbm.shape[0]
    position = lax.axis_index("ctx")
    pairs = []
    for place, index in enumerate((position, ctx_count - 1 - position)):
        columns = pl.ds(pl.multiple_of(index * group // tok * tok, tok), tok)
        pairs += [(decay_hbm.at[:, columns], cut_ref.at[place, :half]), (residue_hbm.at[:, columns], cut_ref.at[place, half:])]
    pairs += [(source, held_ref.at[place]) for place, source in enumerate((value_hbm, gate_hbm, post_hbm))]
    copies = [pltpu.make_async_copy(*pair, sems.at[place]) for place, pair in enumerate(pairs)]
    for copy in copies:
        copy.start()
    sends = []
    for place, target in enumerate((own_hbm, sent_hbm)):
        copies[2 * place].wait()
        copies[2 * place + 1].wait()
        sends.append(pltpu.make_async_copy(cut_ref.at[place], target, out_sems.at[3 + place]))
        sends[-1].start()
    for place, copy in enumerate(copies[4:]):
        copy.wait()
        for first in range(0, width, tok):
            turned = held_ref[place, :, first : first + tok].T
            for part in range(tok // group):
                ready_ref[first // group + part, place] = turned[part * group : (part + 1) * group]
        sends.append(pltpu.make_async_copy(ready_ref.at[:, place], out_hbm.at[:, place], out_sems.at[place]))
        sends[-1].start()
    for send in sends:
        send.wait()


def mirror_rows(value):
    row = lax.broadcasted_iota(jnp.int32, (8, value.shape[1]), 0)
    result = []
    for first in range(value.shape[0] - 8, -1, -8):
        part = value[first : first + 8]
        for shift in (1, 2, 4):
            part = jnp.where(row & shift == 0, pltpu.roll(part, 8 - shift, 0), pltpu.roll(part, shift, 0))
        result.append(part)
    return jnp.concatenate(result, axis=0)


def put_filter(poles, index, turned, time_ref):
    lanes = 128
    rows_all, block = time_ref.shape
    group = turned.shape[0]
    ramp = lax.broadcasted_iota(jnp.int32, (8, lanes), 1).astype(jnp.float32)
    for row in range(0, group, 8):
        rows = slice(row, row + 8)
        rate = turned[rows, index * poles : (index + 1) * poles]
        scale = turned[rows, (2 + index) * poles : (3 + index) * poles] * (jnp.sqrt(rate * (2.0 / poles)) / block)
        slope = rate * -math.log2(math.e)
        sums = [None] * (rows_all // group * block // lanes)
        for pole in range(poles):
            level = jnp.broadcast_to(slope[:, pole : pole + 1], (8, lanes))
            term = scale[:, pole : pole + 1] * jnp.exp2(level * ramp)
            step = jnp.exp2(level * lanes)
            for place in range(len(sums)):
                sums[place] = term if pole == 0 else sums[place] + term
                if place + 1 < len(sums):
                    term = term * step
        for place, total in enumerate(sums):
            lag, lane = divmod(place * lanes, block)
            time_ref[lag * group + row : lag * group + row + 8, lane : lane + lanes] = total


def put_spectra(spec, out_ref):
    blocks, group, twice = out_ref.shape
    block = twice // 2
    sign = (1 - 2 * (lax.broadcasted_iota(jnp.int32, (group, block), 1) % 2)).astype(jnp.float32)
    for lag in range(blocks):
        real = spec[lag * group : (lag + 1) * group, :block]
        imag = spec[lag * group : (lag + 1) * group, block:]
        if lag > 0:
            real = real - sign * spec[(lag - 1) * group : lag * group, block:]
            imag = imag + sign * spec[(lag - 1) * group : lag * group, :block]
        out_ref[lag, :, :block] = real
        out_ref[lag, :, block:] = imag


def filter_kernel(poles, par_ref, out_ref, table_ref, back_ref, time_ref, turned_ref):
    group = out_ref.shape[2]
    put_tables(table_ref, back_ref)
    turned_ref[...] = par_ref[...].T
    turned = turned_ref[pl.ds(pl.multiple_of(lax.axis_index("ctx") * group % turned_ref.shape[0], group), group)]
    put_filter(poles, 0, turned, time_ref.at[0])
    spec = mul3(*halves(time_ref[0]), table_ref)
    put_filter(poles, 1, turned, time_ref.at[1])
    put_spectra(spec, out_ref.at[0])
    put_spectra(mul3(*halves(time_ref[1]), table_ref), out_ref.at[1])


def conv_kernel(
    poles, x_ref, own_ref, par_ref, table_ref, back_ref, out_hbm,
    paired_ref, time_ref, turned_ref, spec_ref, high_ref, low_ref, ready_ref, sems,
):
    turned_ref[...] = par_ref[...].T
    blocks, group, twice = own_ref.shape[1:]
    block = twice // 2
    rows_all = blocks * group
    tall, wide = 16, 128
    pieces = x_ref.shape[0] // blocks
    first = (x_ref.shape[0] - 1 - lax.axis_index("ctx")) * group % turned_ref.shape[0]
    turned = mirror_rows(turned_ref[pl.ds(pl.multiple_of(first, group), group)])

    def rows_of(position):
        return jnp.concatenate(
            [
                jnp.concatenate([x_ref[m * pieces + s, position] for s in range(pieces)], axis=1)
                for m in range(blocks)
            ],
            axis=0,
        )

    def times(index, side, source, row, lane):
        data = []
        for m in range(blocks):
            rows = slice(source + m * group + row, source + m * group + row + tall)
            data.append((spec_ref[rows, lane : lane + wide], spec_ref[rows, block + lane : block + lane + wide]))
        sums = [None] * blocks
        for lag in range(blocks):
            h_ref = (own_ref, paired_ref)[side]
            f_re = h_ref[index, lag, row : row + tall, lane : lane + wide]
            f_im = h_ref[index, lag, row : row + tall, block + lane : block + lane + wide]
            for m in range(blocks - lag):
                target, (d_re, d_im) = (m + lag, data[m]) if side == 0 else (m, data[m + lag])
                if side == 0:
                    real, imag = f_re * d_re - f_im * d_im, f_re * d_im + f_im * d_re
                else:
                    real, imag = f_re * d_re + f_im * d_im, f_re * d_im - f_im * d_re
                if sums[target] is not None:
                    real, imag = sums[target][0] + real, sums[target][1] + imag
                sums[target] = (real, imag)
        return sums

    def keep(target, row, lane, sums):
        for m in range(blocks):
            rows = slice(target + m * group + row, target + m * group + row + tall)
            for part in range(2):
                cols = slice(part * block + lane, part * block + lane + wide)
                high_ref[rows, cols], low_ref[rows, cols] = halves(sums[m][part])

    chunks = [(row, lane) for row in range(0, group, tall) for lane in range(0, block, wide)]

    value = rows_of(0)
    gate = rows_of(1).astype(jnp.float32)
    spec_ref[:rows_all] = mul2(value, table_ref)
    sides = [slice(side * rows_all, (side + 1) * rows_all) for side in range(2)]
    put_filter(poles, 0, turned, time_ref.at[0])
    spec = mul3(*halves(time_ref[0]), table_ref)
    for row, lane in chunks:
        keep(0, row, lane, times(0, 0, 0, row, lane))
    put_spectra(spec, paired_ref.at[0])
    gated = [gate * mul3(high_ref[sides[0]], low_ref[sides[0]], back_ref)]
    put_filter(poles, 1, turned, time_ref.at[1])
    for row, lane in chunks:
        keep(rows_all, row, lane, times(0, 1, 0, row, lane))
    gated.append(gate * mul3(high_ref[sides[1]], low_ref[sides[1]], back_ref))
    spec = mul3(*halves(time_ref[1]), table_ref)
    for side in range(2):
        spec_ref[sides[side]] = mul3(*halves(gated[side]), table_ref)
    put_spectra(spec, paired_ref.at[1])
    for row, lane in chunks:
        ahead, back = times(1, 0, 0, row, lane), times(1, 1, rows_all, row, lane)
        keep(0, row, lane, [(a[0] + b[0], a[1] + b[1]) for a, b in zip(ahead, back)])
    post = rows_of(2)
    tok = block // pieces
    sends = []
    for part in range(2):
        rows = slice(part * rows_all // 2, (part + 1) * rows_all // 2)
        summed = mul3(high_ref[rows], low_ref[rows], back_ref)
        mixed = (post[rows].astype(jnp.float32) * summed).astype(jnp.bfloat16)
        first = part * blocks // 2 * pieces
        for m in range(blocks // 2):
            for s in range(pieces):
                ready_ref[first + m * pieces + s] = mixed[m * group : (m + 1) * group, s * tok : (s + 1) * tok]
        span = pl.ds(first, blocks // 2 * pieces)
        for copy in range(out_hbm.shape[1]):
            sends.append(pltpu.make_async_copy(ready_ref.at[span], out_hbm.at[span, copy], sems.at[part, copy]))
            sends[-1].start()
    for send in sends:
        send.wait()


def project_kernel(mixed_ref, *refs):
    w_refs, (out_hbm, held_ref, ready_ref, sems) = refs[:-4], refs[-4:]
    rows = w_refs[0].shape[0]
    tile = 2 * rows
    position = lax.axis_index("ctx")
    parity = position % 2
    even = pl.multiple_of(parity * rows, rows)
    odd = pl.multiple_of((1 - parity) * rows, rows)
    masks = (0, 1 + parity, 2 - parity, 3)
    ctx_count, tp_count = mixed_ref.shape[:2]
    mixed = jnp.concatenate([mixed_ref[i, z] for z in range(tp_count) for i in range(ctx_count)], axis=0)
    sends = []
    for half in range(2):
        total = mul(jnp.concatenate([w_ref[...] for w_ref in w_refs[4 * half : 4 * half + 4]], axis=0), mixed)
        for pair in range(2):
            place = 2 * half + pair
            held_ref[place, pl.ds(even, rows)] = total[pair * tile : pair * tile + rows]
            held_ref[place, pl.ds(odd, rows)] = total[pair * tile + rows : (pair + 1) * tile]
            ready_ref[place] = held_ref[place].T.astype(jnp.bfloat16)
            columns = pl.ds(pl.multiple_of((position // 2 ^ masks[place]) * tile, tile), tile)
            sends.append(pltpu.make_async_copy(ready_ref.at[place], out_hbm.at[:, columns], sems.at[place]))
            sends[-1].start()
    for send in sends:
        send.wait()


def whole_call(kernel, out_shape, scratch, flops, nbytes, *operands, in_hbm=0, out_hbm=()):
    results = pl.pallas_call(
        kernel,
        out_shape=out_shape,
        in_specs=[
            pl.BlockSpec(memory_space=pltpu.HBM if place < in_hbm else pltpu.VMEM) for place in range(len(operands))
        ],
        out_specs=[
            pl.BlockSpec(memory_space=pltpu.HBM if place in out_hbm else pltpu.VMEM) for place in range(len(out_shape))
        ],
        scratch_shapes=scratch,
        cost_estimate=pl.CostEstimate(flops=flops, bytes_accessed=nbytes, transcendentals=0),
        compiler_params=pltpu.CompilerParams(vmem_limit_bytes=None if in_hbm else 32 * 2**20),
    )(*operands)
    return results if len(out_shape) > 1 else results[0]


def blocked(x_gate, x_post, values, decay, residue, w_out):
    tok, width = x_gate.shape
    ctx_count = lax.axis_size("ctx")
    tp_count = lax.axis_size("tp")
    group = width // ctx_count
    poles = decay.shape[2]
    block = 2 * tok
    blocks = tok * ctx_count // block
    rows, channels = w_out.shape
    half = 2 * poles

    packed, own, mirrored = whole_call(
        pack_kernel,
        (
            jax.ShapeDtypeStruct((ctx_count, 3, group, tok), jnp.bfloat16),
            jax.ShapeDtypeStruct((2 * half, tok), jnp.float32),
            jax.ShapeDtypeStruct((2 * half, tok), jnp.float32),
        ),
        [
            pltpu.VMEM((3, tok, width), jnp.bfloat16),
            pltpu.VMEM((2, 2 * half, tok), jnp.float32),
            pltpu.VMEM((ctx_count, 3, group, tok), jnp.bfloat16),
            pltpu.SemaphoreType.DMA((7,)),
            pltpu.SemaphoreType.DMA((5,)),
        ],
        0,
        6 * tok * width * 2,
        x_gate,
        values,
        x_post,
        jnp.swapaxes(decay, 1, 2).reshape(half, width),
        jnp.swapaxes(residue, 1, 2).reshape(half, width),
        in_hbm=5,
        out_hbm=(0, 1, 2),
    )
    paired = lax.ppermute(mirrored, "tp", [(z, tp_count - 1 - z) for z in range(tp_count)])
    received = lax.all_to_all(packed, "ctx", split_axis=0, concat_axis=0, tiled=True)

    w_late, mirrored = lax.optimization_barrier((w_out, mirrored))

    def cross(block, even_mask, odd_mask):
        return lax.ppermute(block, "ctx", [(i, i ^ (odd_mask if i % 2 else even_mask)) for i in range(ctx_count)])

    w_first = cross(w_late, 2, 4)
    own_spectra, table, back_table = whole_call(
        functools.partial(filter_kernel, poles),
        (
            jax.ShapeDtypeStruct((2, blocks, group, 2 * block), jnp.float32),
            jax.ShapeDtypeStruct((2 * block, 2 * block), jnp.bfloat16),
            jax.ShapeDtypeStruct((4 * block, block), jnp.bfloat16),
        ),
        [
            pltpu.VMEM((2, blocks * group, block), jnp.float32),
            pltpu.VMEM((tok, 2 * half), jnp.float32),
        ],
        2 * 2 * blocks * group * block * 2 * block * 3,
        2 * blocks * group * 2 * block * 4,
        own,
    )
    mixed = whole_call(
        functools.partial(conv_kernel, poles),
        (jax.ShapeDtypeStruct((ctx_count, tp_count, group, tok), jnp.bfloat16),),
        [
            pltpu.VMEM((2, blocks, group, 2 * block), jnp.float32),
            pltpu.VMEM((2, blocks * group, block), jnp.float32),
            pltpu.VMEM((tok, 2 * half), jnp.float32),
            pltpu.VMEM((2 * blocks * group, 2 * block), jnp.float32),
            pltpu.VMEM((2 * blocks * group, 2 * block), jnp.bfloat16),
            pltpu.VMEM((2 * blocks * group, 2 * block), jnp.bfloat16),
            pltpu.VMEM((ctx_count, group, tok), jnp.bfloat16),
            pltpu.SemaphoreType.DMA((2, tp_count)),
        ],
        2 * 8 * blocks * group * block * 2 * block * 3,
        4 * blocks * group * 2 * block * 4,
        received,
        own_spectra,
        paired,
        table,
        back_table,
        out_hbm=(0,),
    )
    mixed, w_first, w_own = lax.optimization_barrier((mixed, w_first, w_out))
    w_third = cross(w_first, 4, 2)
    w_second = cross(w_own, 4, 2)
    w_other = [partner(block, "ctx", 0) for block in (w_own, w_first, w_second, w_third)]
    w_blocks = [w_own, w_other[0], w_first, w_other[2], w_second, w_other[1], w_third, w_other[3]]
    every = lax.all_to_all(
        mixed.reshape(ctx_count * tp_count, group, tok), ("ctx", "tp"), split_axis=0, concat_axis=0, tiled=True
    ).reshape(ctx_count, tp_count, group, tok)
    return whole_call(
        project_kernel,
        (jax.ShapeDtypeStruct((tok, rows * ctx_count), jnp.bfloat16),),
        [
            pltpu.VMEM((ctx_count // 2, 2 * rows, tok), jnp.float32),
            pltpu.VMEM((ctx_count // 2, tok, 2 * rows), jnp.bfloat16),
            pltpu.SemaphoreType.DMA((ctx_count // 2,)),
        ],
        2 * tok * rows * ctx_count * channels,
        2 * rows * ctx_count * channels,
        every,
        *w_blocks,
        out_hbm=(0,),
    )


def local(x_gate, x_post, values, decay, residue, w_out):
    tok, width = x_gate.shape
    ctx_count = lax.axis_size("ctx")
    if tok == 128 and width == 512 and ctx_count == 8 and w_out.shape[0] == 64 and lax.axis_size("tp") == 4:
        return blocked(x_gate, x_post, values, decay, residue, w_out)
    return general(x_gate, x_post, values, decay, residue, w_out)


def solution(mesh):
    in_specs = (
        P("ctx", "tp"),
        P("ctx", "tp"),
        P("ctx", "tp"),
        P(None, "tp", None),
        P(None, "tp", None),
        P(("tp", "ctx"), None),
    )
    out_specs = P("ctx", "tp")
    return jax.shard_map(local, mesh=mesh, in_specs=in_specs, out_specs=out_specs, check_vma=False)
```

profile of v0, /device:TPU:1, one launch (start us, length us, event | category | flops | bytes accessed | tf_op | source)
XLA Modules:
  0.0 40.9 jit_solution(4839438715001479413)
XLA Ops:
  0.0 2.0 %shard_map.64 = (bf16[8,3,64,128]{3,2,1,0:T(8,128)(2,1)}, f32[64,128]{1,0:T(8,128)}, f32[64,128]{1,0:T(8,128)}) custom-call(bf16[128,512]{1,0:T(8,128)(2,1)} %gate_hbm.1, bf16[128,512]{1,0:T(8,128)(2,1)} %value_hbm.1, bf16[128,512]{1,0:T(8,128)(2,1)} %post_hbm.1, f32[32,512]{1,0:T(8,128)} %bitcast.9, f32[32,512]{1,0:T(8,128)} %bitcast.10), custom_call_target="tpu_custom_call" | custom-call | bytes 786432 | tf_op jit(solution)/shard_map/pallas_call | solution.py:509
  2.0 0.0 copy-start
  2.0 0.0 copy-start.2
  2.0 0.0 copy-start.1
  2.1 5.4 %all-to-all-start = ((bf16[8,3,64,128]{3,2,1,0:T(8,128)(2,1)}), bf16[8,3,64,128]{3,2,1,0:T(8,128)(2,1)S(1)}, u32[]{:S(2)}, u32[]{:S(2)}) async-start(bf16[8,3,64,128]{3,2,1,0:T(8,128)(2,1)} %get-tuple-element.15), calls=%async_computation | async-start | bytes 786432 | tf_op jit(solution)/shard_map/all_to_all | solution.py:561
  7.4 0.0 copy-done
  7.4 1.4 %collective-permute-start.1 = (bf16[64,2048]{1,0:T(8,128)(2,1)S(1)}, bf16[64,2048]{1,0:T(8,128)(2,1)S(1)}, u32[]{:S(2)}, u32[]{:S(2)}) collective-permute-start(bf16[64,2048]{1,0:T(8,128)(2,1)S(1)} %copy-done), channel_id=1, source_target_pairs={{0,8},{4,20},{8,0},{12,28},{16,24},{20,4},{24,16},{28,12},{1,9},{5... | collective-permute-start | bytes 786440 | tf_op jit(solution)/shard_map/ppermute | solution.py:566
  8.8 0.0 copy-done.2
  8.8 3.3 %collective-permute-start = (f32[64,128]{1,0:T(8,128)S(1)}, f32[64,128]{1,0:T(8,128)S(1)}, u32[]{:S(2)}, u32[]{:S(2)}) collective-permute-start(f32[64,128]{1,0:T(8,128)S(1)} %copy-done.2), channel_id=1, source_target_pairs={{0,3},{1,2},{2,1},{3,0},{4,7},{5,6},{6,5},{7,4},{8,11},{9,10},{10,... | collective-permute-start | bytes 98312 | tf_op jit(solution)/shard_map/ppermute | solution.py:560
  12.1 0.0 copy-done.1
  12.1 2.4 %shard_map.65 = (f32[2,4,64,512]{3,2,1,0:T(8,128)S(1)}, bf16[512,512]{1,0:T(8,128)(2,1)S(1)}, bf16[1024,256]{1,0:T(8,128)(2,1)S(1)}) custom-call(f32[64,128]{1,0:T(8,128)S(1)} %copy-done.1), custom_call_target="tpu_custom_call" | custom-call | flops 402653184 | bytes 1048576 | tf_op jit(solution)/shard_map/pallas_call | solution.py:509
  14.6 0.0 collective-permute-done.par_ref
  14.6 0.0 all-to-all-done.x_ref
  14.6 4.2 %shard_map.66 = bf16[8,4,64,128]{3,2,1,0:T(8,128)(2,1)} custom-call(bf16[8,3,64,128]{3,2,1,0:T(8,128)(2,1)S(1)} %all-to-all-done.x_ref, f32[2,4,64,512]{3,2,1,0:T(8,128)S(1)} %get-tuple-element.17.own_ref, f32[64,128]{1,0:T(8,128)S(1)} %collective-permute-done.par_ref, bf16[512,512]{1,0:T(8,128)(2,1)S(1)} %get-tuple-element.19.table_ref, ...), custom_call_target="tpu_custom_call" | custom-call | flops 1610612736 | bytes 2097152 | tf_op jit(solution)/shard_map/pallas_call | solution.py:509
  18.8 0.0 collective-permute-done.1.refs_2_
  18.8 5.2 %all-to-all-start.1 = ((bf16[32,64,128]{2,1,0:T(8,128)(2,1)}), bf16[32,64,128]{2,1,0:T(8,128)(2,1)S(1)}, u32[]{:S(2)}, u32[]{:S(2)}) async-start(bf16[32,64,128]{2,1,0:T(8,128)(2,1)} %bitcast.4), calls=%async_computation.1 | async-start | bytes 1048576 | tf_op jit(solution)/shard_map/all_to_all | solution.py:611
  24.0 1.5 %collective-permute-start.3 = (bf16[64,2048]{1,0:T(8,128)(2,1)S(1)}, bf16[64,2048]{1,0:T(8,128)(2,1)S(1)}, u32[]{:S(2)}, u32[]{:S(2)}) collective-permute-start(bf16[64,2048]{1,0:T(8,128)(2,1)S(1)} %copy-done), channel_id=1, source_target_pairs={{0,16},{4,12},{8,24},{12,4},{16,0},{20,28},{24,8},{28,20},{1,17},{... | collective-permute-start | bytes 786440 | tf_op jit(solution)/shard_map/ppermute | solution.py:566
  25.5 0.1 collective-permute-start.6
  25.6 0.8 %collective-permute-start.2 = (bf16[64,2048]{1,0:T(8,128)(2,1)S(1)}, bf16[64,2048]{1,0:T(8,128)(2,1)S(1)}, u32[]{:S(2)}, u32[]{:S(2)}) collective-permute-start(bf16[64,2048]{1,0:T(8,128)(2,1)S(1)} %copy-done), channel_id=1, source_target_pairs={{0,4},{4,0},{8,12},{12,8},{16,20},{20,16},{24,28},{28,24},{1,5},{5... | collective-permute-start | bytes 786440 | tf_op jit(solution)/shard_map/ppermute | solution.py:17
  26.4 0.0 collective-permute-start.5
  26.4 7.0 %collective-permute-done.3.refs_4_ = bf16[64,2048]{1,0:T(8,128)(2,1)S(1)} collective-permute-done((bf16[64,2048]{1,0:T(8,128)(2,1)S(1)}, bf16[64,2048]{1,0:T(8,128)(2,1)S(1)}, u32[]{:S(2)}, u32[]{:S(2)}) %collective-permute-start.3) | collective-permute-done | bytes 262176 | tf_op jit(solution)/shard_map/ppermute | solution.py:566
  33.4 0.9 %collective-permute-start.4 = (bf16[64,2048]{1,0:T(8,128)(2,1)S(1)}, bf16[64,2048]{1,0:T(8,128)(2,1)S(1)}, u32[]{:S(2)}, u32[]{:S(2)}) collective-permute-start(bf16[64,2048]{1,0:T(8,128)(2,1)S(1)} %collective-permute-done.3.refs_4_), channel_id=1, source_target_pairs={{0,4},{4,0},{8,12},{12,8},{16,20},{20,16},{24,28},{28,24},{1,5},{5... | collective-permute-start | bytes 786440 | tf_op jit(solution)/shard_map/ppermute | solution.py:17
  34.4 2.9 %collective-permute-done.6.refs_6_ = bf16[64,2048]{1,0:T(8,128)(2,1)S(1)} collective-permute-done((bf16[64,2048]{1,0:T(8,128)(2,1)S(1)}, bf16[64,2048]{1,0:T(8,128)(2,1)S(1)}, u32[]{:S(2)}, u32[]{:S(2)}) %collective-permute-start.6) | collective-permute-done | bytes 262176 | tf_op jit(solution)/shard_map/ppermute | solution.py:566
  37.3 0.9 %collective-permute-start.7 = (bf16[64,2048]{1,0:T(8,128)(2,1)S(1)}, bf16[64,2048]{1,0:T(8,128)(2,1)S(1)}, u32[]{:S(2)}, u32[]{:S(2)}) collective-permute-start(bf16[64,2048]{1,0:T(8,128)(2,1)S(1)} %collective-permute-done.6.refs_6_), channel_id=1, source_target_pairs={{0,4},{4,0},{8,12},{12,8},{16,20},{20,16},{24,28},{28,24},{1,5},{5... | collective-permute-start | bytes 786440 | tf_op jit(solution)/shard_map/ppermute | solution.py:17
  38.2 0.0 collective-permute-done.2.refs_1_
  38.2 0.0 collective-permute-done.5.refs_5_
  38.2 0.0 collective-permute-done.4.refs_3_
  38.3 1.1 %collective-permute-done.7.refs_7_ = bf16[64,2048]{1,0:T(8,128)(2,1)S(1)} collective-permute-done((bf16[64,2048]{1,0:T(8,128)(2,1)S(1)}, bf16[64,2048]{1,0:T(8,128)(2,1)S(1)}, u32[]{:S(2)}, u32[]{:S(2)}) %collective-permute-start.7) | collective-permute-done | bytes 262176 | tf_op jit(solution)/shard_map/ppermute | solution.py:17
  39.4 0.0 all-to-all-done.1
  39.4 1.5 %shard_map.67 = bf16[128,512]{1,0:T(8,128)(2,1)} custom-call(bf16[8,4,64,128]{3,2,1,0:T(8,128)(2,1)S(1)} %bitcast.8, bf16[64,2048]{1,0:T(8,128)(2,1)S(1)} %copy-done, bf16[64,2048]{1,0:T(8,128)(2,1)S(1)} %collective-permute-done.2.refs_1_, bf16[64,2048]{1,0:T(8,128)(2,1)S(1)} %collective-permute-done.1.refs_2_, ...), custom_call_target="tpu_custom_call" | custom-call | flops 268435456 | bytes 2097152 | tf_op jit(solution)/shard_map/pallas_call | solution.py:509
Async XLA Ops:
  2.0 5.4 %copy-start = (bf16[64,2048]{1,0:T(8,128)(2,1)S(1)}, bf16[64,2048]{1,0:T(8,128)(2,1)}, u32[]{:S(2)}) copy-start(bf16[64,2048]{1,0:T(8,128)(2,1)} %refs_0_) | copy-start | bytes 786436
  2.0 6.8 %copy-start.2 = (f32[64,128]{1,0:T(8,128)S(1)}, f32[64,128]{1,0:T(8,128)}, u32[]{:S(2)}) copy-start(f32[64,128]{1,0:T(8,128)} %get-tuple-element.18) | copy-start | bytes 98308
  2.0 10.1 %copy-start.1 = (f32[64,128]{1,0:T(8,128)S(1)}, f32[64,128]{1,0:T(8,128)}, u32[]{:S(2)}) copy-start(f32[64,128]{1,0:T(8,128)} %get-tuple-element.16.par_ref) | copy-start | bytes 98308
  2.1 12.5 %all-to-all-start = ((bf16[8,3,64,128]{3,2,1,0:T(8,128)(2,1)}), bf16[8,3,64,128]{3,2,1,0:T(8,128)(2,1)S(1)}, u32[]{:S(2)}, u32[]{:S(2)}) async-start(bf16[8,3,64,128]{3,2,1,0:T(8,128)(2,1)} %get-tuple-element.15), calls=%async_computation | async-start | bytes 786432 | tf_op jit(solution)/shard_map/all_to_all | solution.py:561
  7.4 11.4 %collective-permute-start.1 = (bf16[64,2048]{1,0:T(8,128)(2,1)S(1)}, bf16[64,2048]{1,0:T(8,128)(2,1)S(1)}, u32[]{:S(2)}, u32[]{:S(2)}) collective-permute-start(bf16[64,2048]{1,0:T(8,128)(2,1)S(1)} %copy-done), channel_id=1, source_target_pairs={{0,8},{4,20},{8,0},{12,28},{16,24},{20,4},{24,16},{28,12},{1,9},{5... | collective-permute-start | bytes 786440 | tf_op jit(solution)/shard_map/ppermute | solution.py:566
  8.8 5.7 %collective-permute-start = (f32[64,128]{1,0:T(8,128)S(1)}, f32[64,128]{1,0:T(8,128)S(1)}, u32[]{:S(2)}, u32[]{:S(2)}) collective-permute-start(f32[64,128]{1,0:T(8,128)S(1)} %copy-done.2), channel_id=1, source_target_pairs={{0,3},{1,2},{2,1},{3,0},{4,7},{5,6},{6,5},{7,4},{8,11},{9,10},{10,... | collective-permute-start | bytes 98312 | tf_op jit(solution)/shard_map/ppermute | solution.py:560
  18.8 20.6 %all-to-all-start.1 = ((bf16[32,64,128]{2,1,0:T(8,128)(2,1)}), bf16[32,64,128]{2,1,0:T(8,128)(2,1)S(1)}, u32[]{:S(2)}, u32[]{:S(2)}) async-start(bf16[32,64,128]{2,1,0:T(8,128)(2,1)} %bitcast.4), calls=%async_computation.1 | async-start | bytes 1048576 | tf_op jit(solution)/shard_map/all_to_all | solution.py:611
  24.0 9.4 %collective-permute-start.3 = (bf16[64,2048]{1,0:T(8,128)(2,1)S(1)}, bf16[64,2048]{1,0:T(8,128)(2,1)S(1)}, u32[]{:S(2)}, u32[]{:S(2)}) collective-permute-start(bf16[64,2048]{1,0:T(8,128)(2,1)S(1)} %copy-done), channel_id=1, source_target_pairs={{0,16},{4,12},{8,24},{12,4},{16,0},{20,28},{24,8},{28,20},{1,17},{... | collective-permute-start | bytes 786440 | tf_op jit(solution)/shard_map/ppermute | solution.py:566
  25.5 11.8 %collective-permute-start.6 = (bf16[64,2048]{1,0:T(8,128)(2,1)S(1)}, bf16[64,2048]{1,0:T(8,128)(2,1)S(1)}, u32[]{:S(2)}, u32[]{:S(2)}) collective-permute-start(bf16[64,2048]{1,0:T(8,128)(2,1)S(1)} %collective-permute-done.1.refs_2_), channel_id=1, source_target_pairs={{0,16},{4,12},{8,24},{12,4},{16,0},{20,28},{24,8},{28,20},{1,17},{... | collective-permute-start | bytes 786440 | tf_op jit(solution)/shard_map/ppermute | solution.py:566
  25.6 12.7 %collective-permute-start.2 = (bf16[64,2048]{1,0:T(8,128)(2,1)S(1)}, bf16[64,2048]{1,0:T(8,128)(2,1)S(1)}, u32[]{:S(2)}, u32[]{:S(2)}) collective-permute-start(bf16[64,2048]{1,0:T(8,128)(2,1)S(1)} %copy-done), channel_id=1, source_target_pairs={{0,4},{4,0},{8,12},{12,8},{16,20},{20,16},{24,28},{28,24},{1,5},{5... | collective-permute-start | bytes 786440 | tf_op jit(solution)/shard_map/ppermute | solution.py:17
  26.4 11.9 %collective-permute-start.5 = (bf16[64,2048]{1,0:T(8,128)(2,1)S(1)}, bf16[64,2048]{1,0:T(8,128)(2,1)S(1)}, u32[]{:S(2)}, u32[]{:S(2)}) collective-permute-start(bf16[64,2048]{1,0:T(8,128)(2,1)S(1)} %collective-permute-done.1.refs_2_), channel_id=1, source_target_pairs={{0,4},{4,0},{8,12},{12,8},{16,20},{20,16},{24,28},{28,24},{1,5},{5... | collective-permute-start | bytes 786440 | tf_op jit(solution)/shard_map/ppermute | solution.py:17
  33.4 4.8 %collective-permute-start.4 = (bf16[64,2048]{1,0:T(8,128)(2,1)S(1)}, bf16[64,2048]{1,0:T(8,128)(2,1)S(1)}, u32[]{:S(2)}, u32[]{:S(2)}) collective-permute-start(bf16[64,2048]{1,0:T(8,128)(2,1)S(1)} %collective-permute-done.3.refs_4_), channel_id=1, source_target_pairs={{0,4},{4,0},{8,12},{12,8},{16,20},{20,16},{24,28},{28,24},{1,5},{5... | collective-permute-start | bytes 786440 | tf_op jit(solution)/shard_map/ppermute | solution.py:17
  37.3 2.1 %collective-permute-start.7 = (bf16[64,2048]{1,0:T(8,128)(2,1)S(1)}, bf16[64,2048]{1,0:T(8,128)(2,1)S(1)}, u32[]{:S(2)}, u32[]{:S(2)}) collective-permute-start(bf16[64,2048]{1,0:T(8,128)(2,1)S(1)} %collective-permute-done.6.refs_6_), channel_id=1, source_target_pairs={{0,4},{4,0},{8,12},{12,8},{16,20},{20,16},{24,28},{28,24},{1,5},{5... | collective-permute-start | bytes 786440 | tf_op jit(solution)/shard_map/ppermute | solution.py:17
where the time goes:
time: 41.5 us; the launch traced here: 40.9 us
  starting transfers between devices  19.5 us (47%)
  waiting for transfers between devices  11.1 us (27%)
  Pallas kernels  10.2 us (25%)
    pallas_call x4, Pallas kernels, whole_call(): pl.pallas_call(kernel, out_shape=out_shape, in_specs=[pl.BlockSpec(memory...  10.2 us
    ppermute x3, waiting for transfers between devices, cross(): lax.ppermute(block, 'ctx', [(i, i ^ (odd_mask if i % 2 else even_mask)) f...  9.96 us
    all_to_all x1, starting transfers between devices, blocked(): lax.all_to_all(packed, 'ctx', split_axis=0, concat_axis=0, tiled=True)  5.37 us
    all_to_all x1, starting transfers between devices, blocked(): lax.all_to_all(mixed.reshape(ctx_count * tp_count, group, tok), ('ctx', '...  5.2 us
    ppermute x1, starting transfers between devices, blocked(): lax.ppermute(mirrored, 'tp', [(z, tp_count - 1 - z) for z in range(tp_cou...  3.32 us
    ppermute x3, starting transfers between devices, cross(): lax.ppermute(block, 'ctx', [(i, i ^ (odd_mask if i % 2 else even_mask)) f...  2.92 us
    ppermute x4, starting transfers between devices, partner(): return lax.ppermute(value, axis, pairs)  2.71 us
    ppermute x4, waiting for transfers between devices, partner(): return lax.ppermute(value, axis, pairs)  1.16 us
  transfers between devices with their start and end apart: 10, of which 3 were waited for; matrix products, arithmetic and copies ran while one was open for 0% of the time, Pallas kernels for 16%

commit v1 on v0

--- a/solution.py
+++ b/solution.py
@@ -487,7 +487,7 @@
     parity = position % 2
     even = pl.multiple_of(parity * rows, rows)
     odd = pl.multiple_of((1 - parity) * rows, rows)
-    masks = (0, 1 + parity, 2 - parity, 3)
+    masks = (0, 2 - parity, 1 + parity, 3)
     ctx_count, tp_count = mixed_ref.shape[:2]
     mixed = jnp.concatenate([mixed_ref[i, z] for z in range(tp_count) for i in range(ctx_count)], axis=0)
     sends = []
@@ -565,7 +565,7 @@
     def cross(block, even_mask, odd_mask):
         return lax.ppermute(block, "ctx", [(i, i ^ (odd_mask if i % 2 else even_mask)) for i in range(ctx_count)])
 
-    w_first = cross(w_late, 2, 4)
+    w_first = cross(w_late, 4, 2)
     own_spectra, table, back_table = whole_call(
         functools.partial(filter_kernel, poles),
         (
@@ -604,8 +604,8 @@
         out_hbm=(0,),
     )
     mixed, w_first, w_own = lax.optimization_barrier((mixed, w_first, w_out))
-    w_third = cross(w_first, 4, 2)
-    w_second = cross(w_own, 4, 2)
+    w_third = cross(w_first, 2, 4)
+    w_second = cross(w_own, 2, 4)
     w_other = [partner(block, "ctx", 0) for block in (w_own, w_first, w_second, w_third)]
     w_blocks = [w_own, w_other[0], w_first, w_other[2], w_second, w_other[1], w_third, w_other[3]]
     every = lax.all_to_all(

time: 41.5 us -> 41.3 us (level)
  waiting for transfers between devices: 11.1 us -> 12.9 us
  starting transfers between devices: 19.5 us -> 17.9 us
    ppermute x4, starting transfers between devices: 2.71 us -> 0.89 us  [partner(): return lax.ppermute(value, axis, pairs)]
    ppermute x3, waiting for transfers between devices: 9.96 us -> 11.2 us  [cross(): lax.ppermute(block, 'ctx', [(i, i ^ (odd_mask if i % 2 else even_mask)) f...]
  transfers between devices with their start and end apart: 10 -> 10, of which waited for: 3 -> 4; matrix products, arithmetic and copies ran while one was open for 0% -> 0% of each run, Pallas kernels for 16% -> 16%
where the time goes in v1:
time: 41.3 us; the launch traced here: 41 us
  starting transfers between devices  17.9 us (43%)
  waiting for transfers between devices  12.9 us (31%)
  Pallas kernels  10.1 us (24%)
    ppermute x3, waiting for transfers between devices, cross(): lax.ppermute(block, 'ctx', [(i, i ^ (odd_mask if i % 2 else even_mask)) f...  11.2 us
    pallas_call x4, Pallas kernels, whole_call(): pl.pallas_call(kernel, out_shape=out_shape, in_specs=[pl.BlockSpec(memory...  10.1 us
    all_to_all x1, starting transfers between devices, blocked(): lax.all_to_all(mixed.reshape(ctx_count * tp_count, group, tok), ('ctx', '...  5.4 us
    all_to_all x1, starting transfers between devices, blocked(): lax.all_to_all(packed, 'ctx', split_axis=0, concat_axis=0, tiled=True)  5.37 us
    ppermute x1, starting transfers between devices, blocked(): lax.ppermute(mirrored, 'tp', [(z, tp_count - 1 - z) for z in range(tp_cou...  3.32 us
    ppermute x3, starting transfers between devices, cross(): lax.ppermute(block, 'ctx', [(i, i ^ (odd_mask if i % 2 else even_mask)) f...  2.92 us
    ppermute x4, waiting for transfers between devices, partner(): return lax.ppermute(value, axis, pairs)  1.49 us
    ppermute x4, starting transfers between devices, partner(): return lax.ppermute(value, axis, pairs)  0.89 us
  transfers between devices with their start and end apart: 10, of which 4 were waited for; matrix products, arithmetic and copies ran while one was open for 0% of the time, Pallas kernels for 16%

profile of v1, /device:TPU:1, one launch (start us, length us, event | category | flops | bytes accessed | tf_op | source)
XLA Modules:
  0.0 41.0 jit_solution(14140150652694348012)
XLA Ops:
  0.0 2.0 %shard_map.64 = (bf16[8,3,64,128]{3,2,1,0:T(8,128)(2,1)}, f32[64,128]{1,0:T(8,128)}, f32[64,128]{1,0:T(8,128)}) custom-call(bf16[128,512]{1,0:T(8,128)(2,1)} %gate_hbm.1, bf16[128,512]{1,0:T(8,128)(2,1)} %value_hbm.1, bf16[128,512]{1,0:T(8,128)(2,1)} %post_hbm.1, f32[32,512]{1,0:T(8,128)} %bitcast.9, f32[32,512]{1,0:T(8,128)} %bitcast.10), custom_call_target="tpu_custom_call" | custom-call | bytes 786432 | tf_op jit(solution)/shard_map/pallas_call | solution.py:509
  2.0 0.0 copy-start
  2.0 0.0 copy-start.2
  2.0 0.0 copy-start.1
  2.1 5.4 %all-to-all-start = ((bf16[8,3,64,128]{3,2,1,0:T(8,128)(2,1)}), bf16[8,3,64,128]{3,2,1,0:T(8,128)(2,1)S(1)}, u32[]{:S(2)}, u32[]{:S(2)}) async-start(bf16[8,3,64,128]{3,2,1,0:T(8,128)(2,1)} %get-tuple-element.15), calls=%async_computation | async-start | bytes 786432 | tf_op jit(solution)/shard_map/all_to_all | solution.py:561
  7.4 0.0 copy-done
  7.4 1.4 %collective-permute-start.1 = (bf16[64,2048]{1,0:T(8,128)(2,1)S(1)}, bf16[64,2048]{1,0:T(8,128)(2,1)S(1)}, u32[]{:S(2)}, u32[]{:S(2)}) collective-permute-start(bf16[64,2048]{1,0:T(8,128)(2,1)S(1)} %copy-done), channel_id=1, source_target_pairs={{0,16},{4,12},{8,24},{12,4},{16,0},{20,28},{24,8},{28,20},{1,17},{... | collective-permute-start | bytes 786440 | tf_op jit(solution)/shard_map/ppermute | solution.py:566
  8.8 0.0 copy-done.2
  8.8 3.3 %collective-permute-start = (f32[64,128]{1,0:T(8,128)S(1)}, f32[64,128]{1,0:T(8,128)S(1)}, u32[]{:S(2)}, u32[]{:S(2)}) collective-permute-start(f32[64,128]{1,0:T(8,128)S(1)} %copy-done.2), channel_id=1, source_target_pairs={{0,3},{1,2},{2,1},{3,0},{4,7},{5,6},{6,5},{7,4},{8,11},{9,10},{10,... | collective-permute-start | bytes 98312 | tf_op jit(solution)/shard_map/ppermute | solution.py:560
  12.1 0.0 copy-done.1
  12.1 2.4 %shard_map.65 = (f32[2,4,64,512]{3,2,1,0:T(8,128)S(1)}, bf16[512,512]{1,0:T(8,128)(2,1)S(1)}, bf16[1024,256]{1,0:T(8,128)(2,1)S(1)}) custom-call(f32[64,128]{1,0:T(8,128)S(1)} %copy-done.1), custom_call_target="tpu_custom_call" | custom-call | flops 402653184 | bytes 1048576 | tf_op jit(solution)/shard_map/pallas_call | solution.py:509
  14.5 0.0 collective-permute-done.par_ref
  14.6 0.0 all-to-all-done.x_ref
  14.6 4.2 %shard_map.66 = bf16[8,4,64,128]{3,2,1,0:T(8,128)(2,1)} custom-call(bf16[8,3,64,128]{3,2,1,0:T(8,128)(2,1)S(1)} %all-to-all-done.x_ref, f32[2,4,64,512]{3,2,1,0:T(8,128)S(1)} %get-tuple-element.17.own_ref, f32[64,128]{1,0:T(8,128)S(1)} %collective-permute-done.par_ref, bf16[512,512]{1,0:T(8,128)(2,1)S(1)} %get-tuple-element.19.table_ref, ...), custom_call_target="tpu_custom_call" | custom-call | flops 1610612736 | bytes 2097152 | tf_op jit(solution)/shard_map/pallas_call | solution.py:509
  18.8 0.0 collective-permute-done.1.refs_2_
  18.8 5.4 %all-to-all-start.1 = ((bf16[32,64,128]{2,1,0:T(8,128)(2,1)}), bf16[32,64,128]{2,1,0:T(8,128)(2,1)S(1)}, u32[]{:S(2)}, u32[]{:S(2)}) async-start(bf16[32,64,128]{2,1,0:T(8,128)(2,1)} %bitcast.4), calls=%async_computation.1 | async-start | bytes 1048576 | tf_op jit(solution)/shard_map/all_to_all | solution.py:611
  24.2 1.5 %collective-permute-start.3 = (bf16[64,2048]{1,0:T(8,128)(2,1)S(1)}, bf16[64,2048]{1,0:T(8,128)(2,1)S(1)}, u32[]{:S(2)}, u32[]{:S(2)}) collective-permute-start(bf16[64,2048]{1,0:T(8,128)(2,1)S(1)} %copy-done), channel_id=1, source_target_pairs={{0,8},{4,20},{8,0},{12,28},{16,24},{20,4},{24,16},{28,12},{1,9},{5... | collective-permute-start | bytes 786440 | tf_op jit(solution)/shard_map/ppermute | solution.py:566
  25.7 0.1 collective-permute-start.6
  25.7 0.8 %collective-permute-start.2 = (bf16[64,2048]{1,0:T(8,128)(2,1)S(1)}, bf16[64,2048]{1,0:T(8,128)(2,1)S(1)}, u32[]{:S(2)}, u32[]{:S(2)}) collective-permute-start(bf16[64,2048]{1,0:T(8,128)(2,1)S(1)} %copy-done), channel_id=1, source_target_pairs={{0,4},{4,0},{8,12},{12,8},{16,20},{20,16},{24,28},{28,24},{1,5},{5... | collective-permute-start | bytes 786440 | tf_op jit(solution)/shard_map/ppermute | solution.py:17
  26.6 0.0 collective-permute-start.5
  26.6 7.4 %collective-permute-done.3.refs_4_ = bf16[64,2048]{1,0:T(8,128)(2,1)S(1)} collective-permute-done((bf16[64,2048]{1,0:T(8,128)(2,1)S(1)}, bf16[64,2048]{1,0:T(8,128)(2,1)S(1)}, u32[]{:S(2)}, u32[]{:S(2)}) %collective-permute-start.3) | collective-permute-done | bytes 262176 | tf_op jit(solution)/shard_map/ppermute | solution.py:566
  34.0 0.0 collective-permute-start.4
  34.0 3.8 %collective-permute-done.6.refs_6_ = bf16[64,2048]{1,0:T(8,128)(2,1)S(1)} collective-permute-done((bf16[64,2048]{1,0:T(8,128)(2,1)S(1)}, bf16[64,2048]{1,0:T(8,128)(2,1)S(1)}, u32[]{:S(2)}, u32[]{:S(2)}) %collective-permute-start.6) | collective-permute-done | bytes 262176 | tf_op jit(solution)/shard_map/ppermute | solution.py:566
  37.8 0.0 collective-permute-start.7
  37.9 0.0 collective-permute-done.2.refs_1_
  37.9 0.0 collective-permute-done.5.refs_5_
  37.9 0.0 collective-permute-done.4.refs_3_
  37.9 1.5 %collective-permute-done.7.refs_7_ = bf16[64,2048]{1,0:T(8,128)(2,1)S(1)} collective-permute-done((bf16[64,2048]{1,0:T(8,128)(2,1)S(1)}, bf16[64,2048]{1,0:T(8,128)(2,1)S(1)}, u32[]{:S(2)}, u32[]{:S(2)}) %collective-permute-start.7) | collective-permute-done | bytes 262176 | tf_op jit(solution)/shard_map/ppermute | solution.py:17
  39.4 0.1 all-to-all-done.1
  39.5 1.5 %shard_map.67 = bf16[128,512]{1,0:T(8,128)(2,1)} custom-call(bf16[8,4,64,128]{3,2,1,0:T(8,128)(2,1)S(1)} %bitcast.8, bf16[64,2048]{1,0:T(8,128)(2,1)S(1)} %copy-done, bf16[64,2048]{1,0:T(8,128)(2,1)S(1)} %collective-permute-done.2.refs_1_, bf16[64,2048]{1,0:T(8,128)(2,1)S(1)} %collective-permute-done.1.refs_2_, ...), custom_call_target="tpu_custom_call" | custom-call | flops 268435456 | bytes 2097152 | tf_op jit(solution)/shard_map/pallas_call | solution.py:509
Async XLA Ops:
  2.0 5.4 %copy-start = (bf16[64,2048]{1,0:T(8,128)(2,1)S(1)}, bf16[64,2048]{1,0:T(8,128)(2,1)}, u32[]{:S(2)}) copy-start(bf16[64,2048]{1,0:T(8,128)(2,1)} %refs_0_) | copy-start | bytes 786436
  2.0 6.8 %copy-start.2 = (f32[64,128]{1,0:T(8,128)S(1)}, f32[64,128]{1,0:T(8,128)}, u32[]{:S(2)}) copy-start(f32[64,128]{1,0:T(8,128)} %get-tuple-element.18) | copy-start | bytes 98308
  2.0 10.1 %copy-start.1 = (f32[64,128]{1,0:T(8,128)S(1)}, f32[64,128]{1,0:T(8,128)}, u32[]{:S(2)}) copy-start(f32[64,128]{1,0:T(8,128)} %get-tuple-element.16.par_ref) | copy-start | bytes 98308
  2.1 12.5 %all-to-all-start = ((bf16[8,3,64,128]{3,2,1,0:T(8,128)(2,1)}), bf16[8,3,64,128]{3,2,1,0:T(8,128)(2,1)S(1)}, u32[]{:S(2)}, u32[]{:S(2)}) async-start(bf16[8,3,64,128]{3,2,1,0:T(8,128)(2,1)} %get-tuple-element.15), calls=%async_computation | async-start | bytes 786432 | tf_op jit(solution)/shard_map/all_to_all | solution.py:561
  7.4 11.4 %collective-permute-start.1 = (bf16[64,2048]{1,0:T(8,128)(2,1)S(1)}, bf16[64,2048]{1,0:T(8,128)(2,1)S(1)}, u32[]{:S(2)}, u32[]{:S(2)}) collective-permute-start(bf16[64,2048]{1,0:T(8,128)(2,1)S(1)} %copy-done), channel_id=1, source_target_pairs={{0,16},{4,12},{8,24},{12,4},{16,0},{20,28},{24,8},{28,20},{1,17},{... | collective-permute-start | bytes 786440 | tf_op jit(solution)/shard_map/ppermute | solution.py:566
  8.8 5.7 %collective-permute-start = (f32[64,128]{1,0:T(8,128)S(1)}, f32[64,128]{1,0:T(8,128)S(1)}, u32[]{:S(2)}, u32[]{:S(2)}) collective-permute-start(f32[64,128]{1,0:T(8,128)S(1)} %copy-done.2), channel_id=1, source_target_pairs={{0,3},{1,2},{2,1},{3,0},{4,7},{5,6},{6,5},{7,4},{8,11},{9,10},{10,... | collective-permute-start | bytes 98312 | tf_op jit(solution)/shard_map/ppermute | solution.py:560
  18.8 20.7 %all-to-all-start.1 = ((bf16[32,64,128]{2,1,0:T(8,128)(2,1)}), bf16[32,64,128]{2,1,0:T(8,128)(2,1)S(1)}, u32[]{:S(2)}, u32[]{:S(2)}) async-start(bf16[32,64,128]{2,1,0:T(8,128)(2,1)} %bitcast.4), calls=%async_computation.1 | async-start | bytes 1048576 | tf_op jit(solution)/shard_map/all_to_all | solution.py:611
  24.2 9.8 %collective-permute-start.3 = (bf16[64,2048]{1,0:T(8,128)(2,1)S(1)}, bf16[64,2048]{1,0:T(8,128)(2,1)S(1)}, u32[]{:S(2)}, u32[]{:S(2)}) collective-permute-start(bf16[64,2048]{1,0:T(8,128)(2,1)S(1)} %copy-done), channel_id=1, source_target_pairs={{0,8},{4,20},{8,0},{12,28},{16,24},{20,4},{24,16},{28,12},{1,9},{5... | collective-permute-start | bytes 786440 | tf_op jit(solution)/shard_map/ppermute | solution.py:566
  25.7 12.2 %collective-permute-start.6 = (bf16[64,2048]{1,0:T(8,128)(2,1)S(1)}, bf16[64,2048]{1,0:T(8,128)(2,1)S(1)}, u32[]{:S(2)}, u32[]{:S(2)}) collective-permute-start(bf16[64,2048]{1,0:T(8,128)(2,1)S(1)} %collective-permute-done.1.refs_2_), channel_id=1, source_target_pairs={{0,8},{4,20},{8,0},{12,28},{16,24},{20,4},{24,16},{28,12},{1,9},{5... | collective-permute-start | bytes 786440 | tf_op jit(solution)/shard_map/ppermute | solution.py:566
  25.7 12.1 %collective-permute-start.2 = (bf16[64,2048]{1,0:T(8,128)(2,1)S(1)}, bf16[64,2048]{1,0:T(8,128)(2,1)S(1)}, u32[]{:S(2)}, u32[]{:S(2)}) collective-permute-start(bf16[64,2048]{1,0:T(8,128)(2,1)S(1)} %copy-done), channel_id=1, source_target_pairs={{0,4},{4,0},{8,12},{12,8},{16,20},{20,16},{24,28},{28,24},{1,5},{5... | collective-permute-start | bytes 786440 | tf_op jit(solution)/shard_map/ppermute | solution.py:17
  26.6 11.3 %collective-permute-start.5 = (bf16[64,2048]{1,0:T(8,128)(2,1)S(1)}, bf16[64,2048]{1,0:T(8,128)(2,1)S(1)}, u32[]{:S(2)}, u32[]{:S(2)}) collective-permute-start(bf16[64,2048]{1,0:T(8,128)(2,1)S(1)} %collective-permute-done.1.refs_2_), channel_id=1, source_target_pairs={{0,4},{4,0},{8,12},{12,8},{16,20},{20,16},{24,28},{28,24},{1,5},{5... | collective-permute-start | bytes 786440 | tf_op jit(solution)/shard_map/ppermute | solution.py:17
  34.0 3.9 %collective-permute-start.4 = (bf16[64,2048]{1,0:T(8,128)(2,1)S(1)}, bf16[64,2048]{1,0:T(8,128)(2,1)S(1)}, u32[]{:S(2)}, u32[]{:S(2)}) collective-permute-start(bf16[64,2048]{1,0:T(8,128)(2,1)S(1)} %collective-permute-done.3.refs_4_), channel_id=1, source_target_pairs={{0,4},{4,0},{8,12},{12,8},{16,20},{20,16},{24,28},{28,24},{1,5},{5... | collective-permute-start | bytes 786440 | tf_op jit(solution)/shard_map/ppermute | solution.py:17
  37.8 1.5 %collective-permute-start.7 = (bf16[64,2048]{1,0:T(8,128)(2,1)S(1)}, bf16[64,2048]{1,0:T(8,128)(2,1)S(1)}, u32[]{:S(2)}, u32[]{:S(2)}) collective-permute-start(bf16[64,2048]{1,0:T(8,128)(2,1)S(1)} %collective-permute-done.6.refs_6_), channel_id=1, source_target_pairs={{0,4},{4,0},{8,12},{12,8},{16,20},{20,16},{24,28},{28,24},{1,5},{5... | collective-permute-start | bytes 786440 | tf_op jit(solution)/shard_map/ppermute | solution.py:17
